TPU v7x, 32 devices: a whole 2x2x4 slice. The times are simulated.
32 devices in a mesh: outer: 2 (over x), inner: 16 (over z, y, core).
Axes of the slice: x: 2, y: 2, z: 4, core: 2. Of those that a mesh axis runs over, the one named last changes fastest.
Arguments:
- query_stream: float32 [16384, 128], P(('outer', 'inner')), may hold values from -6 to 6
- key_stream: float32 [16384, 128], P(('outer', 'inner')), may hold values from -6 to 6
- value_stream: float32 [16384, 128], P(('outer', 'inner')), may hold values from -6 to 6
- filter_taps: float32 [16384, 128], P(('outer', 'inner')), may hold values from -1.6 to 1.6
- skip_gain: float32 [128], replicated, may hold values from -1 to 1
- short_weights: float32 [3, 3, 128], replicated, may hold values from -3 to 3
- cotangent: float32 [16384, 128], P(('outer', 'inner')), may hold values from -10 to 10
Outputs:
- gated_output: float32 [16384, 128], P(('outer', 'inner'))
- stream_grads: float32 [3, 16384, 128], P(None, ('outer', 'inner'))
- filter_grad: float32 [16384, 128], P(('outer', 'inner'))
- tap_grads: float32 [3, 3, 128], replicated
- skip_grad: float32 [128], replicated
All inputs are finite; a program needn't handle non-finite values.
Results may differ from a plain program's by a relative error of at most 0.0003.
Values sent between devices are 32-bit elements; how exact they have to be, the bound alone decides.
A program may use at most 64 MiB of HBM per device.

v0:
```python
import functools
import math

import jax
import jax.numpy as jnp
import ml_dtypes
import numpy as np
from jax import lax
from jax.experimental import pallas as pl
from jax.experimental.pallas import tpu as pltpu
from jax.sharding import PartitionSpec as P

MESH = pl.DeviceIdType.MESH

exact_mode = lax.Precision.HIGHEST


def passed_along(block, axis, distance):
    devices = range(lax.axis_size(axis))
    route = [(i - distance, i) for i in devices if i - distance in devices]
    return lax.ppermute(block, axis, route)


def unit_angles(counts_table, period):
    return 2.0 * math.pi / period * (counts_table % period).astype(jnp.float32)


def turned(real_part, imag_part, cosine, sine, sign):
    return (
        real_part * cosine - sign * imag_part * sine,
        imag_part * cosine + sign * real_part * sine,
    )


def applied(formula, angles, real_part, imag_part, sign):
    cosine = jnp.cos(angles)
    sine = jnp.sin(angles)
    cos_real = jnp.einsum(formula, cosine, real_part, precision=exact_mode)
    cos_imag = jnp.einsum(formula, cosine, imag_part, precision=exact_mode)
    sin_real = jnp.einsum(formula, sine, real_part, precision=exact_mode)
    sin_imag = jnp.einsum(formula, sine, imag_part, precision=exact_mode)
    return (cos_real - sign * sin_imag, cos_imag + sign * sin_real)


def sequence_blocks(tiles):
    groups, devices, tile_size = tiles.shape
    shaped = tiles.reshape(groups, lax.axis_size("outer"), lax.axis_size("inner"), 1, 1, tile_size)
    moved = lax.all_to_all(
        lax.all_to_all(shaped, "outer", split_axis=1, concat_axis=3, tiled=True),
        "inner",
        split_axis=2,
        concat_axis=4,
        tiled=True,
    )
    return moved.reshape(groups, devices, tile_size)


def spectral_blocks(tiles):
    groups, devices, tile_size = tiles.shape
    shaped = tiles.reshape(groups, lax.axis_size("outer"), lax.axis_size("inner"), 1, 1, tile_size)
    moved = lax.all_to_all(
        lax.all_to_all(shaped, "outer", split_axis=1, concat_axis=3, tiled=True),
        "inner",
        split_axis=2,
        concat_axis=4,
        tiled=True,
    )
    return moved.reshape(groups, devices, tile_size)


def self_position():
    return lax.axis_index("outer") * lax.axis_size("inner") + lax.axis_index("inner")


def local_forward(real_part, imag_part):
    members, pairs, row_count, channels = real_part.shape
    second = row_count // 16
    first_index = jnp.arange(16, dtype=jnp.int32)
    second_index = jnp.arange(second, dtype=jnp.int32)
    real_part = real_part.reshape(members, pairs, 16, second, channels)
    imag_part = imag_part.reshape(members, pairs, 16, second, channels)
    first_angles = unit_angles(first_index[:, None] * first_index[None, :], 16)
    real_part, imag_part = applied("ka,mtacx->mtkcx", first_angles, real_part, imag_part, -1.0)
    twiddle = unit_angles(first_index[:, None] * second_index[None, :], row_count)[:, :, None]
    real_part, imag_part = turned(real_part, imag_part, jnp.cos(twiddle), jnp.sin(twiddle), -1.0)
    second_angles = unit_angles(second_index[:, None] * second_index[None, :], second)
    real_part, imag_part = applied("qc,mtkcx->mtqkx", second_angles, real_part, imag_part, -1.0)
    return (
        real_part.reshape(members, pairs, row_count, channels),
        imag_part.reshape(members, pairs, row_count, channels),
    )


def local_inverse(real_part, imag_part):
    members, pairs, row_count, channels = real_part.shape
    second = row_count // 16
    first_index = jnp.arange(16, dtype=jnp.int32)
    second_index = jnp.arange(second, dtype=jnp.int32)
    real_part = real_part.reshape(members, pairs, second, 16, channels)
    imag_part = imag_part.reshape(members, pairs, second, 16, channels)
    second_angles = unit_angles(second_index[:, None] * second_index[None, :], second)
    real_part, imag_part = applied("cq,mtqkx->mtckx", second_angles, real_part, imag_part, 1.0)
    twiddle = unit_angles(second_index[:, None] * first_index[None, :], row_count)[:, :, None]
    real_part, imag_part = turned(real_part, imag_part, jnp.cos(twiddle), jnp.sin(twiddle), 1.0)
    first_angles = unit_angles(first_index[:, None] * first_index[None, :], 16)
    real_part, imag_part = applied("ak,mtckx->mtacx", first_angles, real_part, imag_part, 1.0)
    return (
        real_part.reshape(members, pairs, row_count, channels),
        imag_part.reshape(members, pairs, row_count, channels),
    )


def fourier_forward(signals):
    members, row_count, channels = signals.shape
    devices = lax.axis_size("outer") * lax.axis_size("inner")
    tile_rows = row_count // devices
    length = 2 * row_count * devices
    columns = sequence_blocks(signals.reshape(members, devices, tile_rows * channels))
    parity = jnp.arange(2, dtype=jnp.int32)
    target = jnp.arange(devices, dtype=jnp.int32)
    frequency = 2 * target[None, :] + parity[:, None]
    angles = unit_angles(frequency[:, :, None] * target[None, None, :], 2 * devices)
    first_real = jnp.einsum("tdb,mbx->mtdx", jnp.cos(angles), columns, precision=exact_mode)
    first_imag = -jnp.einsum("tdb,mbx->mtdx", jnp.sin(angles), columns, precision=exact_mode)
    first_real = first_real.reshape(members, 2, devices, tile_rows, channels)
    first_imag = first_imag.reshape(members, 2, devices, tile_rows, channels)
    offset = self_position() * tile_rows + jnp.arange(tile_rows, dtype=jnp.int32)
    twiddle = unit_angles(frequency[:, :, None] * offset[None, None, :], length)[:, :, :, None]
    first_real, first_imag = turned(
        first_real, first_imag, jnp.cos(twiddle), jnp.sin(twiddle), -1.0
    )
    stacked = jnp.stack([first_real, first_imag], axis=1).reshape(
        members * 4, devices, tile_rows * channels
    )
    spread = spectral_blocks(stacked).reshape(members, 2, 2, row_count, channels)
    return local_forward(spread[:, 0], spread[:, 1])


def fourier_inverse(real_part, imag_part):
    members, pairs, row_count, channels = real_part.shape
    devices = lax.axis_size("outer") * lax.axis_size("inner")
    tile_rows = row_count // devices
    length = 2 * row_count * devices
    real_part, imag_part = local_inverse(real_part, imag_part)
    parity = jnp.arange(2, dtype=jnp.int32)
    frequency = 2 * self_position() + parity
    twiddle = unit_angles(
        frequency[:, None] * jnp.arange(row_count, dtype=jnp.int32)[None, :], length
    )[:, :, None]
    real_part, imag_part = turned(real_part, imag_part, jnp.cos(twiddle), jnp.sin(twiddle), 1.0)
    stacked = jnp.stack([real_part, imag_part], axis=1).reshape(
        members * 4, devices, tile_rows * channels
    )
    gathered = spectral_blocks(stacked).reshape(members, 2, 2, devices, tile_rows * channels)
    target = jnp.arange(devices, dtype=jnp.int32)
    angles = unit_angles(
        target[:, None, None] * (2 * target[None, None, :] + parity[None, :, None]), 2 * devices
    )
    cosine = jnp.cos(angles)
    sine = jnp.sin(angles)
    scale = 1.0 / length
    real_out = (
        jnp.einsum("btd,mtdx->mbx", cosine, gathered[:, 0], precision=exact_mode)
        - jnp.einsum("btd,mtdx->mbx", sine, gathered[:, 1], precision=exact_mode)
    ) * scale
    imag_out = real_out[:0]
    return (real_out, imag_out)


def on_device(
    query_stream, key_stream, value_stream, filter_taps, skip_gain, short_weights, cotangent
):
    row_count, channels = query_stream.shape
    devices = lax.axis_size("outer") * lax.axis_size("inner")
    streams = jnp.stack([query_stream, key_stream, value_stream])
    earlier = passed_along(streams[:, row_count - 2 :, :], ("outer", "inner"), 1)
    ahead = jnp.concatenate([earlier, streams], axis=1)
    lag_one = ahead[:, 1 : row_count + 1]
    lag_two = ahead[:, 0:row_count]
    mixed = (
        short_weights[:, 0:1] * streams
        + short_weights[:, 1:2] * lag_one
        + short_weights[:, 2:3] * lag_two
    )
    product = mixed[1] * mixed[2]
    upstream = cotangent * mixed[0]
    spec_real, spec_imag = fourier_forward(jnp.stack([filter_taps, product, upstream]))
    filter_real, product_real, upstream_real = (spec_real[0], spec_real[1], spec_real[2])
    filter_imag, product_imag, upstream_imag = (spec_imag[0], spec_imag[1], spec_imag[2])
    causal_real = filter_real * product_real - filter_imag * product_imag
    causal_imag = filter_real * product_imag + filter_imag * product_real
    back_real = filter_real * upstream_real + filter_imag * upstream_imag
    back_imag = filter_real * upstream_imag - filter_imag * upstream_real
    grad_real = product_real * upstream_real + product_imag * upstream_imag
    grad_imag = product_real * upstream_imag - product_imag * upstream_real
    real_out, imag_out = fourier_inverse(
        jnp.stack([causal_real, back_real, grad_real]),
        jnp.stack([causal_imag, back_imag, grad_imag]),
    )
    longs = sequence_blocks(real_out).reshape(3, row_count, channels)
    summed = longs[0] + skip_gain * product
    gated_output = mixed[0] * summed
    backward = longs[1] + skip_gain * upstream
    grads = jnp.stack([cotangent * summed, backward * mixed[2], backward * mixed[1]])
    later = passed_along(grads[:, 0:2, :], ("outer", "inner"), -1)
    behind = jnp.concatenate([grads, later], axis=1)
    stream_grads = (
        short_weights[:, 0:1] * grads
        + short_weights[:, 1:2] * behind[:, 1 : row_count + 1]
        + short_weights[:, 2:3] * behind[:, 2 : row_count + 2]
    )
    tap_terms = jnp.stack(
        [
            jnp.sum(grads * streams, axis=1),
            jnp.sum(grads * lag_one, axis=1),
            jnp.sum(grads * lag_two, axis=1),
        ],
        axis=1,
    )
    skip_terms = jnp.sum(upstream * product, axis=0)
    tap_total, skip_total = lax.psum((tap_terms, skip_terms), ("outer", "inner"))
    factor = 1.0 / math.sqrt(row_count * devices)
    return (gated_output, stream_grads, longs[2] * factor, tap_total * factor, skip_total * factor)


LANES = 128


def halves(table):
    high = table.astype(ml_dtypes.bfloat16)
    low = (table - high.astype(np.float64)).astype(ml_dtypes.bfloat16)
    return high, low


def fourier_tables(devices, pieces):
    outer_size = devices * pieces
    length = outer_size * LANES
    place = np.arange(outer_size)
    place = (place % devices) * pieces + place // devices
    low = np.arange(outer_size)
    lane = np.arange(LANES)
    angle = 2.0 * np.pi / (4 * outer_size) * ((4 * low[:, None] + 1) * place[None, :] % (4 * outer_size))
    rows = np.concatenate([np.cos(angle), -np.sin(angle)], axis=0)
    row_high, row_low = halves(rows)
    forward_rows = np.concatenate([row_high, row_low, row_high], axis=1)
    back_high, back_low = halves(rows.T / length)
    inverse_rows = np.concatenate([back_high, back_low, back_high], axis=1)
    turn = 2.0 * np.pi / (4 * length) * ((4 * low[:, None] + 1) * lane[None, :] % (4 * length))
    twiddle = np.stack([np.cos(turn), -np.sin(turn)]).astype(np.float32)
    angle = 2.0 * np.pi / LANES * (lane[:, None] * lane[None, :] % LANES)
    cosine, sine = np.cos(angle), -np.sin(angle)
    forward = np.block([[cosine, sine], [-sine, cosine]])
    inverse = np.block([[cosine, -sine], [sine, cosine]])
    columns = np.stack([*halves(forward), *halves(inverse)])
    return forward_rows, inverse_rows, columns, twiddle


def split(value):
    high = value.astype(jnp.bfloat16)
    return high, (value - high.astype(jnp.float32)).astype(jnp.bfloat16)


def dot(left, right):
    return jnp.dot(left, right, preferred_element_type=jnp.float32)


def three_dots(value, high_table, low_table):
    high, low = split(value)
    return dot(high, high_table) + dot(high, low_table) + dot(low, high_table)


def kernel(
    outer_count,
    inner_count,
    query_ref,
    key_ref,
    value_ref,
    taps_ref,
    gain_ref,
    weights_ref,
    cotangent_ref,
    forward_ref,
    inverse_ref,
    columns_ref,
    twiddle_ref,
    gated_ref,
    stream_grads_ref,
    filter_grad_ref,
    tap_grads_ref,
    skip_grad_ref,
    streams,
    mixed,
    product,
    upstream,
    grads,
    sent,
    arrived,
    spectra,
    sent_back,
    arrived_back,
    sums,
    sums_in,
    totals,
    totals_in,
    send_sems,
    recv_sems,
    halo_send,
    halo_recv,
    sum_send,
    sum_recv,
):
    devices = outer_count * inner_count
    row_count = query_ref.shape[0]
    pieces = row_count // LANES
    owned = LANES // devices
    tile = owned * pieces
    outer_size = devices * pieces
    my_outer = lax.axis_index("outer")
    my_inner = lax.axis_index("inner")
    me = my_outer * inner_count + my_inner

    def device(index):
        return (index // inner_count, index % inner_count)

    barrier = pltpu.get_barrier_semaphore()

    def greet(step, carry):
        pl.semaphore_signal(
            barrier, inc=1, device_id=device((me + step) % devices), device_id_type=MESH
        )
        return carry

    lax.fori_loop(1, devices, greet, 0)
    pl.semaphore_wait(barrier, devices - 1)

    following = (me + 1) % devices
    preceding = (me + devices - 1) % devices
    stream_refs = (query_ref, key_ref, value_ref)
    halo_copies = [
        pltpu.make_async_remote_copy(
            src_ref=stream_refs[s].at[pl.ds(row_count - 8, 8), :],
            dst_ref=streams.at[s, pl.ds(0, 8), :],
            send_sem=halo_send.at[s],
            recv_sem=halo_recv.at[s],
            device_id=device(following),
            device_id_type=MESH,
        )
        for s in range(3)
    ]
    for copy in halo_copies:
        copy.start()

    def mine():
        return pl.ds(pl.multiple_of(me * tile, tile), tile)

    def exchange(source, target, group, signal):
        def send(step, carry):
            peer = (me + step) % devices
            pltpu.make_async_remote_copy(
                src_ref=source.at[signal, pl.ds(pl.multiple_of(peer * tile, tile), tile), :],
                dst_ref=target.at[signal, mine(), :],
                send_sem=send_sems.at[group, signal],
                recv_sem=recv_sems.at[group, signal],
                device_id=device(peer),
                device_id_type=MESH,
            ).start()
            return carry

        lax.fori_loop(1, devices, send, 0)
        target[signal, mine(), :] = source[signal, mine(), :]

    def all_but_one(buffer, signal):
        return buffer.at[signal, pl.ds(0, (devices - 1) * tile), :]

    def received(target, group, signal):
        view = all_but_one(target, signal)
        pltpu.make_async_copy(view, view, recv_sems.at[group, signal]).wait()

    def drained(source, group, signal):
        view = all_but_one(source, signal)
        pltpu.make_async_copy(view, view, send_sems.at[group, signal]).wait()

    def put(block, signal, piece):
        sent[signal, pl.ds(piece, LANES, stride=pieces), :] = block.T

    for piece in range(pieces):
        put(taps_ref[pl.ds(piece * LANES, LANES), :], 0, piece)
    exchange(sent, arrived, 0, 0)

    for s in range(3):
        streams[s, pl.ds(8, row_count), :] = stream_refs[s][...]
    for copy in halo_copies:
        copy.wait()
    for s in range(3):
        streams[s, pl.ds(0, 8), :] = jnp.where(me > 0, streams[s, pl.ds(0, 8), :], 0.0)
    def mix(s, piece):
        base = 8 + piece * LANES
        return (
            weights_ref[s, 0:1, :] * streams[s, pl.ds(base, LANES), :]
            + weights_ref[s, 1:2, :] * streams[s, pl.ds(base - 1, LANES), :]
            + weights_ref[s, 2:3, :] * streams[s, pl.ds(base - 2, LANES), :]
        )

    for piece in range(pieces):
        rows = pl.ds(piece * LANES, LANES)
        key, value = mix(1, piece), mix(2, piece)
        mixed[1, rows, :] = key
        mixed[2, rows, :] = value
        product[rows, :] = key * value
        put(key * value, 1, piece)
    exchange(sent, arrived, 0, 1)
    skip_sum = jnp.zeros((1, LANES), jnp.float32)
    for piece in range(pieces):
        rows = pl.ds(piece * LANES, LANES)
        query = mix(0, piece)
        mixed[0, rows, :] = query
        rising = cotangent_ref[rows, :] * query
        upstream[rows, :] = rising
        put(rising, 2, piece)
        skip_sum += jnp.sum(rising * product[rows, :], axis=0, keepdims=True)
    exchange(sent, arrived, 0, 2)

    twiddle_real = twiddle_ref[0]
    twiddle_imag = twiddle_ref[1]

    def transform(signal):
        received(arrived, 0, signal)
        for c in range(owned):
            block = jnp.concatenate(
                [
                    arrived[signal, pl.ds(c * pieces + piece, devices, stride=tile), :]
                    for piece in range(pieces)
                ],
                axis=0,
            )
            high, low = split(block)
            first = dot(forward_ref[...], jnp.concatenate([high, high, low], axis=0))
            real, imag = first[:outer_size], first[outer_size:]
            turned_block = jnp.concatenate(
                [
                    real * twiddle_real - imag * twiddle_imag,
                    real * twiddle_imag + imag * twiddle_real,
                ],
                axis=1,
            )
            spectra[signal, c] = three_dots(turned_block, columns_ref[0], columns_ref[1])

    def back(first, second, conjugated, signal):
        for c in range(owned):
            one, two = spectra[first, c], spectra[second, c]
            one_real, one_imag = one[:, :LANES], one[:, LANES:]
            two_real, two_imag = two[:, :LANES], two[:, LANES:]
            if conjugated:
                real = one_real * two_real + one_imag * two_imag
                imag = one_real * two_imag - one_imag * two_real
            else:
                real = one_real * two_real - one_imag * two_imag
                imag = one_real * two_imag + one_imag * two_real
            inner = three_dots(
                jnp.concatenate([real, imag], axis=1), columns_ref[2], columns_ref[3]
            )
            real, imag = inner[:, :LANES], inner[:, LANES:]
            turned_block = jnp.concatenate(
                [
                    real * twiddle_real + imag * twiddle_imag,
                    imag * twiddle_real - real * twiddle_imag,
                ],
                axis=0,
            )
            high, low = split(turned_block)
            block = dot(inverse_ref[...], jnp.concatenate([high, high, low], axis=0))
            for piece in range(pieces):
                sent_back[signal, pl.ds(c * pieces + piece, devices, stride=tile), :] = block[
                    piece * devices : (piece + 1) * devices
                ]
        exchange(sent_back, arrived_back, 1, signal)

    transform(0)
    transform(1)
    back(0, 1, False, 0)
    transform(2)
    back(0, 2, True, 1)
    back(1, 2, True, 2)

    def piece_of(signal, piece):
        return arrived_back[signal, pl.ds(piece, LANES, stride=pieces), :].T

    gain = gain_ref[...]
    tap_sums = [[jnp.zeros((1, LANES), jnp.float32) for _ in range(3)] for _ in range(3)]

    def add_taps(s, piece, values):
        for j in range(3):
            earlier = streams[s, pl.ds(8 + piece * LANES - j, LANES), :]
            tap_sums[s][j] += jnp.sum(values * earlier, axis=0, keepdims=True)

    received(arrived_back, 1, 0)
    for piece in range(pieces):
        rows = pl.ds(piece * LANES, LANES)
        summed = piece_of(0, piece) + gain * product[rows, :]
        gated_ref[rows, :] = mixed[0, rows, :] * summed
        values = cotangent_ref[rows, :] * summed
        grads[0, rows, :] = values
        add_taps(0, piece, values)
    received(arrived_back, 1, 1)
    for piece in range(pieces):
        rows = pl.ds(piece * LANES, LANES)
        backward = piece_of(1, piece) + gain * upstream[rows, :]
        for s in (1, 2):
            values = backward * mixed[3 - s, rows, :]
            grads[s, rows, :] = values
            add_taps(s, piece, values)

    grad_halo = pltpu.make_async_remote_copy(
        src_ref=grads.at[:, pl.ds(0, 8), :],
        dst_ref=grads.at[:, pl.ds(row_count, 8), :],
        send_sem=halo_send.at[3],
        recv_sem=halo_recv.at[3],
        device_id=device(preceding),
        device_id_type=MESH,
    )
    grad_halo.start()

    group = 4 if inner_count % 4 == 0 else inner_count
    places = inner_count // group
    planes = outer_count * group
    my_place = my_inner // group
    my_member = my_outer * group + my_inner % group
    listed = [tap_sums[s][j] for s in range(3) for j in range(3)] + [skip_sum]
    for at, row in enumerate(listed):
        sums[at : at + 1, :] = row
    sums[10:16, :] = jnp.zeros((6, LANES), jnp.float32)
    sums_in[my_member] = sums[...]

    def send_sums(step, carry):
        member = (my_member + step) % planes
        pltpu.make_async_remote_copy(
            src_ref=sums,
            dst_ref=sums_in.at[my_member],
            send_sem=sum_send.at[0],
            recv_sem=sum_recv.at[0],
            device_id=(member // group, my_place * group + member % group),
            device_id_type=MESH,
        ).start()
        return carry

    lax.fori_loop(1, planes, send_sums, 0)

    def stream_grad(s, start, size):
        return (
            weights_ref[s, 0:1, :] * grads[s, pl.ds(start, size), :]
            + weights_ref[s, 1:2, :] * grads[s, pl.ds(start + 1, size), :]
            + weights_ref[s, 2:3, :] * grads[s, pl.ds(start + 2, size), :]
        )

    for s in range(3):
        for start in range(0, row_count, LANES):
            size = min(LANES, row_count - 8 - start)
            stream_grads_ref[s, pl.ds(start, size), :] = stream_grad(s, start, size)

    def take(view, semaphore):
        pltpu.make_async_copy(view, view, semaphore).wait()

    take(sums_in.at[pl.ds(0, planes - 1)], sum_recv.at[0])
    total = sums_in[0]
    for member in range(1, planes):
        total += sums_in[member]
    totals[...] = total
    totals_in[my_place] = total

    def send_totals(step, carry):
        place = (my_place + step) % places
        pltpu.make_async_remote_copy(
            src_ref=totals,
            dst_ref=totals_in.at[my_place],
            send_sem=sum_send.at[1],
            recv_sem=sum_recv.at[1],
            device_id=(my_outer, place * group + my_inner % group),
            device_id_type=MESH,
        ).start()
        return carry

    lax.fori_loop(1, places, send_totals, 0)

    grad_halo.wait()
    grads[:, pl.ds(row_count, 8), :] = jnp.where(
        me < devices - 1, grads[:, pl.ds(row_count, 8), :], 0.0
    )
    for s in range(3):
        stream_grads_ref[s, pl.ds(row_count - 8, 8), :] = stream_grad(s, row_count - 8, 8)

    factor = 1.0 / math.sqrt(row_count * devices)
    received(arrived_back, 1, 2)
    for piece in range(pieces):
        filter_grad_ref[pl.ds(piece * LANES, LANES), :] = piece_of(2, piece) * factor

    if places > 1:
        take(totals_in.at[pl.ds(0, places - 1)], sum_recv.at[1])
    total = totals_in[0]
    for place in range(1, places):
        total += totals_in[place]
    total = total * factor
    for s in range(3):
        tap_grads_ref[s] = total[3 * s : 3 * s + 3, :]
    skip_grad_ref[...] = total[9:10, :]

    for signal in range(3):
        drained(sent, 0, signal)
        drained(sent_back, 1, signal)
    take(sums_in.at[pl.ds(0, planes - 1)], sum_send.at[0])
    if places > 1:
        take(totals_in.at[pl.ds(0, places - 1)], sum_send.at[1])


def by_channel(
    outer_count,
    inner_count,
    query_stream,
    key_stream,
    value_stream,
    filter_taps,
    skip_gain,
    short_weights,
    cotangent,
):
    row_count, channels = query_stream.shape
    devices = outer_count * inner_count
    pieces = row_count // LANES
    owned = channels // devices
    tables = fourier_tables(devices, pieces)
    group = 4 if inner_count % 4 == 0 else inner_count
    whole = pltpu.VMEM((row_count, channels), jnp.float32)
    three = pltpu.VMEM((3, row_count, channels), jnp.float32)
    padded = pltpu.VMEM((3, row_count + 8, channels), jnp.float32)
    vmem = pl.BlockSpec(memory_space=pltpu.VMEM)
    outs = pl.pallas_call(
        functools.partial(kernel, outer_count, inner_count),
        out_shape=(
            jax.ShapeDtypeStruct((row_count, channels), jnp.float32),
            jax.ShapeDtypeStruct((3, row_count, channels), jnp.float32),
            jax.ShapeDtypeStruct((row_count, channels), jnp.float32),
            jax.ShapeDtypeStruct((3, 3, channels), jnp.float32),
            jax.ShapeDtypeStruct((1, channels), jnp.float32),
        ),
        in_specs=[vmem] * 11,
        out_specs=(vmem,) * 5,
        scratch_shapes=[
            padded,
            three,
            whole,
            whole,
            padded,
            three,
            three,
            pltpu.VMEM((3, owned, devices * pieces, 2 * LANES), jnp.float32),
            three,
            three,
            pltpu.VMEM((16, channels), jnp.float32),
            pltpu.VMEM((outer_count * group, 16, channels), jnp.float32),
            pltpu.VMEM((16, channels), jnp.float32),
            pltpu.VMEM((inner_count // group, 16, channels), jnp.float32),
            pltpu.SemaphoreType.DMA((2, 3)),
            pltpu.SemaphoreType.DMA((2, 3)),
            pltpu.SemaphoreType.DMA((4,)),
            pltpu.SemaphoreType.DMA((4,)),
            pltpu.SemaphoreType.DMA((2,)),
            pltpu.SemaphoreType.DMA((2,)),
        ],
        compiler_params=pltpu.CompilerParams(
            collective_id=0, has_side_effects=True, vmem_limit_bytes=48 * 1024 * 1024
        ),
    )(
        query_stream,
        key_stream,
        value_stream,
        filter_taps,
        skip_gain.reshape(1, channels),
        short_weights,
        cotangent,
        *(jnp.asarray(table) for table in tables),
    )
    return (*outs[:4], outs[4].reshape(channels))


def either_plan(outer_count, inner_count, query_stream, *others):
    row_count, channels = query_stream.shape
    devices = outer_count * inner_count
    even = (
        channels == LANES
        and row_count % LANES == 0
        and channels % devices == 0
        and (channels // devices) * (row_count // LANES) % 8 == 0
        and devices % 8 == 0
    )
    if even:
        return by_channel(outer_count, inner_count, query_stream, *others)
    return on_device(query_stream, *others)


def solution(mesh):
    placed = (
        P(("outer", "inner"), None),
        P(("outer", "inner"), None),
        P(("outer", "inner"), None),
        P(("outer", "inner"), None),
        P(),
        P(),
        P(("outer", "inner"), None),
    )
    return jax.shard_map(
        functools.partial(either_plan, mesh.shape["outer"], mesh.shape["inner"]),
        mesh=mesh,
        in_specs=placed,
        out_specs=(
            P(("outer", "inner"), None),
            P(None, ("outer", "inner"), None),
            P(("outer", "inner"), None),
            P(),
            P(),
        ),
        check_vma=False,
    )
```

profile of v0, /device:TPU:0, one launch (start us, length us, event | category | flops | bytes accessed | tf_op | source)
XLA Modules:
  0.0 62.4 jit_solution(2811450707558128379)
XLA Ops:
  0.6 0.0 copy-start.10
  0.6 0.6 %copy-done.10 = f32[128]{0:T(128)S(1)} copy-done((f32[128]{0:T(128)S(1)}, f32[128]{0:T(128)}, u32[]{:S(2)}) %copy-start.10) | copy-done | bytes 536
  1.3 0.0 copy-start
  1.3 1.0 %copy-done = bf16[4,256,256]{2,1,0:T(8,128)(2,1)S(1)} copy-done((bf16[4,256,256]{2,1,0:T(8,128)(2,1)S(1)}, bf16[4,256,256]{2,1,0:T(8,128)(2,1)}, u32[]{:S(2)}) %copy-start) | copy-done | bytes 524312
  2.3 0.0 copy-start.1
  2.3 0.9 %copy-done.1 = f32[512,128]{1,0:T(8,128)S(1)} copy-done((f32[512,128]{1,0:T(8,128)S(1)}, f32[512,128]{1,0:T(8,128)}, u32[]{:S(2)}) %copy-start.1) | copy-done | bytes 262168
  3.3 0.0 copy-start.2
  3.3 0.9 %copy-done.2 = f32[512,128]{1,0:T(8,128)S(1)} copy-done((f32[512,128]{1,0:T(8,128)S(1)}, f32[512,128]{1,0:T(8,128)}, u32[]{:S(2)}) %copy-start.2) | copy-done | bytes 262168
  4.2 0.0 copy-start.3
  4.2 0.9 %copy-done.3 = f32[512,128]{1,0:T(8,128)S(1)} copy-done((f32[512,128]{1,0:T(8,128)S(1)}, f32[512,128]{1,0:T(8,128)}, u32[]{:S(2)}) %copy-start.3) | copy-done | bytes 262168
  5.2 0.0 copy-start.4
  5.2 0.9 %copy-done.4 = f32[512,128]{1,0:T(8,128)S(1)} copy-done((f32[512,128]{1,0:T(8,128)S(1)}, f32[512,128]{1,0:T(8,128)}, u32[]{:S(2)}) %copy-start.4) | copy-done | bytes 262168
  6.1 0.0 copy-start.5
  6.1 0.9 %copy-done.5 = f32[512,128]{1,0:T(8,128)S(1)} copy-done((f32[512,128]{1,0:T(8,128)S(1)}, f32[512,128]{1,0:T(8,128)}, u32[]{:S(2)}) %copy-start.5) | copy-done | bytes 262168
  7.1 0.0 copy-start.6
  7.1 0.9 %copy-done.6 = bf16[128,768]{1,0:T(8,128)(2,1)S(1)} copy-done((bf16[128,768]{1,0:T(8,128)(2,1)S(1)}, bf16[128,768]{1,0:T(8,128)(2,1)}, u32[]{:S(2)}) %copy-start.6) | copy-done | bytes 196632
  8.0 0.0 copy-start.7
  8.0 0.9 %copy-done.7 = bf16[256,384]{1,0:T(8,128)(2,1)S(1)} copy-done((bf16[256,384]{1,0:T(8,128)(2,1)S(1)}, bf16[256,384]{1,0:T(8,128)(2,1)}, u32[]{:S(2)}) %copy-start.7) | copy-done | bytes 196632
  8.9 0.0 copy-start.8
  8.9 0.9 %copy-done.8 = f32[2,128,128]{2,1,0:T(8,128)S(1)} copy-done((f32[2,128,128]{2,1,0:T(8,128)S(1)}, f32[2,128,128]{2,1,0:T(8,128)}, u32[]{:S(2)}) %copy-start.8) | copy-done | bytes 131096
  9.8 0.0 copy-start.9
  9.8 0.7 %copy-done.9 = f32[3,3,128]{2,1,0:T(4,128)S(1)} copy-done((f32[3,3,128]{2,1,0:T(4,128)S(1)}, f32[3,3,128]{2,1,0:T(4,128)}, u32[]{:S(2)}) %copy-start.9) | copy-done | bytes 4632
  10.5 48.5 %shard_map.146 = (f32[512,128]{1,0:T(8,128)S(1)}, f32[3,512,128]{2,1,0:T(8,128)S(1)}, f32[512,128]{1,0:T(8,128)S(1)}, f32[3,3,128]{2,1,0:T(4,128)S(1)}, f32[1,128]{1,0:T(1,128)S(1)}) custom-call(f32[512,128]{1,0:T(8,128)S(1)} %copy-done.1, f32[512,128]{1,0:T(8,128)S(1)} %copy-done.2, f32[512,128]{1,0:T(8,128)S(1)} %copy-done.3, f32[512,128]{1,0:T(8,128)S(1)} %copy-done.4, ...), custom_call_target="tpu_custom_call" | custom-call | tf_op jit(solution)/shard_map/pallas_call | solution.py:635
  59.0 0.7 %copy.21 = f32[512,128]{1,0:T(8,128)} copy(f32[512,128]{1,0:T(8,128)S(1)} %get-tuple-element.20) | data formatting | bytes 524288
  59.7 0.9 %copy.22 = f32[3,512,128]{2,1,0:T(8,128)} copy(f32[3,512,128]{2,1,0:T(8,128)S(1)} %get-tuple-element.21) | data formatting | bytes 1572864
  60.6 0.7 %copy.23 = f32[512,128]{1,0:T(8,128)} copy(f32[512,128]{1,0:T(8,128)S(1)} %get-tuple-element.22) | data formatting | bytes 524288
  61.3 0.6 copy.24
  61.9 0.5 copy.25
Async XLA Ops:
  0.6 0.7 %copy-start.10 = (f32[128]{0:T(128)S(1)}, f32[128]{0:T(128)}, u32[]{:S(2)}) copy-start(f32[128]{0:T(128)} %param.15) | copy-start | bytes 1540
  1.3 1.0 %copy-start = (bf16[4,256,256]{2,1,0:T(8,128)(2,1)S(1)}, bf16[4,256,256]{2,1,0:T(8,128)(2,1)}, u32[]{:S(2)}) copy-start(bf16[4,256,256]{2,1,0:T(8,128)(2,1)} %constant.10.clone.columns_ref) | copy-start | bytes 1572868
  2.3 0.9 %copy-start.1 = (f32[512,128]{1,0:T(8,128)S(1)}, f32[512,128]{1,0:T(8,128)}, u32[]{:S(2)}) copy-start(f32[512,128]{1,0:T(8,128)} %query_ref.1) | copy-start | bytes 786436
  3.3 0.9 %copy-start.2 = (f32[512,128]{1,0:T(8,128)S(1)}, f32[512,128]{1,0:T(8,128)}, u32[]{:S(2)}) copy-start(f32[512,128]{1,0:T(8,128)} %key_ref.1) | copy-start | bytes 786436
  4.2 0.9 %copy-start.3 = (f32[512,128]{1,0:T(8,128)S(1)}, f32[512,128]{1,0:T(8,128)}, u32[]{:S(2)}) copy-start(f32[512,128]{1,0:T(8,128)} %value_ref.1) | copy-start | bytes 786436
  5.2 0.9 %copy-start.4 = (f32[512,128]{1,0:T(8,128)S(1)}, f32[512,128]{1,0:T(8,128)}, u32[]{:S(2)}) copy-start(f32[512,128]{1,0:T(8,128)} %taps_ref.1) | copy-start | bytes 786436
  6.1 0.9 %copy-start.5 = (f32[512,128]{1,0:T(8,128)S(1)}, f32[512,128]{1,0:T(8,128)}, u32[]{:S(2)}) copy-start(f32[512,128]{1,0:T(8,128)} %cotangent_ref.1) | copy-start | bytes 786436
  7.1 0.9 %copy-start.6 = (bf16[128,768]{1,0:T(8,128)(2,1)S(1)}, bf16[128,768]{1,0:T(8,128)(2,1)}, u32[]{:S(2)}) copy-start(bf16[128,768]{1,0:T(8,128)(2,1)} %constant.9.clone.inverse_ref) | copy-start | bytes 589828
  8.0 0.9 %copy-start.7 = (bf16[256,384]{1,0:T(8,128)(2,1)S(1)}, bf16[256,384]{1,0:T(8,128)(2,1)}, u32[]{:S(2)}) copy-start(bf16[256,384]{1,0:T(8,128)(2,1)} %constant.8.clone.forward_ref) | copy-start | bytes 589828
  8.9 0.9 %copy-start.8 = (f32[2,128,128]{2,1,0:T(8,128)S(1)}, f32[2,128,128]{2,1,0:T(8,128)}, u32[]{:S(2)}) copy-start(f32[2,128,128]{2,1,0:T(8,128)} %constant.11.clone.twiddle_ref) | copy-start | bytes 393220
  9.8 0.7 %copy-start.9 = (f32[3,3,128]{2,1,0:T(4,128)S(1)}, f32[3,3,128]{2,1,0:T(4,128)}, u32[]{:S(2)}) copy-start(f32[3,3,128]{2,1,0:T(4,128)} %weights_ref.1) | copy-start | bytes 13828
where the time goes:
time: 62.9 us; the launch traced here: 62.4 us
  Pallas kernels  48.5 us (77%)
  local copies, waits for them, and re-layouts  13.3 us (21%)
  between operations  0.66 us (1%)
    pallas_call x1, Pallas kernels, by_channel(): pl.pallas_call(functools.partial(kernel, outer_count, inner_count), out_s...  48.5 us
    unnamed x27, local copies, waits for them, and re-layouts  13.3 us

commit v1 on v0

--- a/solution.py
+++ b/solution.py
@@ -272,17 +272,17 @@
 def kernel(
     outer_count,
     inner_count,
-    query_ref,
-    key_ref,
-    value_ref,
-    taps_ref,
-    gain_ref,
-    weights_ref,
-    cotangent_ref,
-    forward_ref,
-    inverse_ref,
-    columns_ref,
-    twiddle_ref,
+    query_hbm,
+    key_hbm,
+    value_hbm,
+    taps_hbm,
+    gain_hbm,
+    weights_hbm,
+    cotangent_hbm,
+    forward_hbm,
+    inverse_hbm,
+    columns_hbm,
+    twiddle_hbm,
     gated_ref,
     stream_grads_ref,
     filter_grad_ref,
@@ -308,9 +308,18 @@
     halo_recv,
     sum_send,
     sum_recv,
+    taps_ref,
+    gain_ref,
+    weights_ref,
+    cotangent_ref,
+    forward_ref,
+    inverse_ref,
+    columns_ref,
+    twiddle_ref,
+    load_sems,
 ):
     devices = outer_count * inner_count
-    row_count = query_ref.shape[0]
+    row_count = query_hbm.shape[0]
     pieces = row_count // LANES
     owned = LANES // devices
     tile = owned * pieces
@@ -331,14 +340,32 @@
         return carry
 
     lax.fori_loop(1, devices, greet, 0)
-    pl.semaphore_wait(barrier, devices - 1)
+
+    stream_hbms = (query_hbm, key_hbm, value_hbm)
+    loads = {}
+    for at, (name, source, target) in enumerate(
+        [
+            ("taps", taps_hbm, taps_ref),
+            ("key", key_hbm, streams.at[1, pl.ds(8, row_count), :]),
+            ("value", value_hbm, streams.at[2, pl.ds(8, row_count), :]),
+            ("query", query_hbm, streams.at[0, pl.ds(8, row_count), :]),
+            ("weights", weights_hbm, weights_ref),
+            ("cotangent", cotangent_hbm, cotangent_ref),
+            ("forward", forward_hbm, forward_ref),
+            ("twiddle", twiddle_hbm, twiddle_ref),
+            ("columns", columns_hbm, columns_ref),
+            ("inverse", inverse_hbm, inverse_ref),
+            ("gain", gain_hbm, gain_ref),
+        ]
+    ):
+        loads[name] = pltpu.make_async_copy(source, target, load_sems.at[at])
+        loads[name].start()
 
     following = (me + 1) % devices
     preceding = (me + devices - 1) % devices
-    stream_refs = (query_ref, key_ref, value_ref)
     halo_copies = [
         pltpu.make_async_remote_copy(
-            src_ref=stream_refs[s].at[pl.ds(row_count - 8, 8), :],
+            src_ref=stream_hbms[s].at[pl.ds(row_count - 8, 8), :],
             dst_ref=streams.at[s, pl.ds(0, 8), :],
             send_sem=halo_send.at[s],
             recv_sem=halo_recv.at[s],
@@ -347,15 +374,26 @@
         )
         for s in range(3)
     ]
-    for copy in halo_copies:
-        copy.start()
+
+    group = 4 if inner_count % 4 == 0 else inner_count
+    places = inner_count // group
+    planes = outer_count * group
+    my_place = my_inner // group
+    my_member = my_outer * group + my_inner % group
+
+    def peer_at(step):
+        place = (my_place + places - step % places) % places
+        turn = ((step - 1) // places + 1) % planes
+        outer = (my_outer + turn) % outer_count
+        member = (my_inner + turn // outer_count) % group
+        return outer * inner_count + place * group + member
 
     def mine():
         return pl.ds(pl.multiple_of(me * tile, tile), tile)
 
     def exchange(source, target, group, signal):
         def send(step, carry):
-            peer = (me + step) % devices
+            peer = peer_at(step)
             pltpu.make_async_remote_copy(
                 src_ref=source.at[signal, pl.ds(pl.multiple_of(peer * tile, tile), tile), :],
                 dst_ref=target.at[signal, mine(), :],
@@ -383,16 +421,22 @@
     def put(block, signal, piece):
         sent[signal, pl.ds(piece, LANES, stride=pieces), :] = block.T
 
+    loads["taps"].wait()
     for piece in range(pieces):
         put(taps_ref[pl.ds(piece * LANES, LANES), :], 0, piece)
+    pl.semaphore_wait(barrier, devices - 1)
+
+    for copy in halo_copies:
+        copy.start()
     exchange(sent, arrived, 0, 0)
 
-    for s in range(3):
-        streams[s, pl.ds(8, row_count), :] = stream_refs[s][...]
+    for name in ("key", "value", "query", "weights", "cotangent"):
+        loads[name].wait()
     for copy in halo_copies:
         copy.wait()
     for s in range(3):
         streams[s, pl.ds(0, 8), :] = jnp.where(me > 0, streams[s, pl.ds(0, 8), :], 0.0)
+
     def mix(s, piece):
         base = 8 + piece * LANES
         return (
@@ -420,6 +464,8 @@
         skip_sum += jnp.sum(rising * product[rows, :], axis=0, keepdims=True)
     exchange(sent, arrived, 0, 2)
 
+    for name in ("forward", "twiddle", "columns", "inverse", "gain"):
+        loads[name].wait()
     twiddle_real = twiddle_ref[0]
     twiddle_imag = twiddle_ref[1]
 
@@ -520,11 +566,6 @@
     )
     grad_halo.start()
 
-    group = 4 if inner_count % 4 == 0 else inner_count
-    places = inner_count // group
-    planes = outer_count * group
-    my_place = my_inner // group
-    my_member = my_outer * group + my_inner % group
     listed = [tap_sums[s][j] for s in range(3) for j in range(3)] + [skip_sum]
     for at, row in enumerate(listed):
         sums[at : at + 1, :] = row
@@ -609,6 +650,18 @@
     take(sums_in.at[pl.ds(0, planes - 1)], sum_send.at[0])
     if places > 1:
         take(totals_in.at[pl.ds(0, places - 1)], sum_send.at[1])
+
+
+def store_kernel(*refs):
+    sources, targets, sems = refs[:5], refs[5:10], refs[10]
+    copies = [
+        pltpu.make_async_copy(source, target, sems.at[at])
+        for at, (source, target) in enumerate(zip(sources, targets))
+    ]
+    for copy in copies:
+        copy.start()
+    for copy in copies:
+        copy.wait()
 
 
 def by_channel(
@@ -641,7 +694,7 @@
             jax.ShapeDtypeStruct((3, 3, channels), jnp.float32),
             jax.ShapeDtypeStruct((1, channels), jnp.float32),
         ),
-        in_specs=[vmem] * 11,
+        in_specs=[pl.BlockSpec(memory_space=pltpu.HBM)] * 11,
         out_specs=(vmem,) * 5,
         scratch_shapes=[
             padded,
@@ -664,9 +717,15 @@
             pltpu.SemaphoreType.DMA((4,)),
             pltpu.SemaphoreType.DMA((2,)),
             pltpu.SemaphoreType.DMA((2,)),
+            whole,
+            pltpu.VMEM((1, channels), jnp.float32),
+            pltpu.VMEM(short_weights.shape, jnp.float32),
+            whole,
+            *(pltpu.VMEM(table.shape, table.dtype) for table in tables),
+            pltpu.SemaphoreType.DMA((11,)),
         ],
         compiler_params=pltpu.CompilerParams(
-            collective_id=0, has_side_effects=True, vmem_limit_bytes=48 * 1024 * 1024
+            collective_id=0, has_side_effects=True, vmem_limit_bytes=63 * 1024 * 1024
         ),
     )(
         query_stream,
@@ -678,6 +737,13 @@
         cotangent,
         *(jnp.asarray(table) for table in tables),
     )
+    outs = pl.pallas_call(
+        store_kernel,
+        out_shape=tuple(jax.ShapeDtypeStruct(out.shape, out.dtype) for out in outs),
+        in_specs=[vmem] * 5,
+        out_specs=(pl.BlockSpec(memory_space=pltpu.HBM),) * 5,
+        scratch_shapes=[pltpu.SemaphoreType.DMA((5,))],
+    )(*outs)
     return (*outs[:4], outs[4].reshape(channels))
 
 

time: 62.9 us -> 52.3 us (0.83)
  local copies, waits for them, and re-layouts: 13.3 us -> 0 us
  Pallas kernels: 48.5 us -> 51.5 us
    unnamed x27 -> x0, local copies, waits for them, and re-layouts: 13.3 us -> none
    pallas_call x0 -> x1, Pallas kernels: none -> 2.38 us  [by_channel(): pl.pallas_call(store_kernel, out_shape=tuple((jax.ShapeDtypeStruct(out.sh...]
    pallas_call x1, Pallas kernels: 48.5 us -> 49.1 us  [by_channel(): pl.pallas_call(functools.partial(kernel, outer_count, inner_count), out_s...]
where the time goes in v1:
time: 52.3 us; the launch traced here: 52.2 us
  Pallas kernels  51.5 us (98%)
  between operations  0.64 us (1%)
    pallas_call x1, Pallas kernels, by_channel(): pl.pallas_call(functools.partial(kernel, outer_count, inner_count), out_s...  49.1 us
    pallas_call x1, Pallas kernels, by_channel(): pl.pallas_call(store_kernel, out_shape=tuple((jax.ShapeDtypeStruct(out.sh...  2.38 us

profile of v1, /device:TPU:0, one launch (start us, length us, event | category | flops | bytes accessed | tf_op | source)
XLA Modules:
  0.0 52.2 jit_solution(12591213824633501559)
XLA Ops:
  0.6 49.1 %shard_map.146 = (f32[512,128]{1,0:T(8,128)}, f32[3,512,128]{2,1,0:T(8,128)}, f32[512,128]{1,0:T(8,128)}, f32[3,3,128]{2,1,0:T(4,128)}, f32[1,128]{1,0:T(1,128)}) custom-call(f32[512,128]{1,0:T(8,128)} %query_hbm.1, f32[512,128]{1,0:T(8,128)} %key_hbm.1, f32[512,128]{1,0:T(8,128)} %value_hbm.1, f32[512,128]{1,0:T(8,128)} %taps_hbm.1, f32[1,128]{1,0:T(1,128)} %bitcast.2, ...), custom_call_target="tpu_custom_call" | custom-call | tf_op jit(solution)/shard_map/pallas_call | solution.py:688
  49.8 2.4 %shard_map.147 = (f32[512,128]{1,0:T(8,128)}, f32[3,512,128]{2,1,0:T(8,128)}, f32[512,128]{1,0:T(8,128)}, f32[3,3,128]{2,1,0:T(4,128)}, f32[1,128]{1,0:T(1,128)}) custom-call(f32[512,128]{1,0:T(8,128)} %get-tuple-element.15.refs_0_, f32[3,512,128]{2,1,0:T(8,128)} %get-tuple-element.16.refs_1_, f32[512,128]{1,0:T(8,128)} %get-tuple-element.17.refs_2_, ...), custom_call_target="tpu_custom_call" | custom-call | tf_op jit(solution)/shard_map/pallas_call | solution.py:740

commit v2 on v1

--- a/solution.py
+++ b/solution.py
@@ -381,30 +381,34 @@
     my_place = my_inner // group
     my_member = my_outer * group + my_inner % group
 
-    def peer_at(step):
-        place = (my_place + places - step % places) % places
-        turn = ((step - 1) // places + 1) % planes
-        outer = (my_outer + turn) % outer_count
-        member = (my_inner + turn // outer_count) % group
-        return outer * inner_count + place * group + member
+    near_places = [lax.rem(my_place + places - shift, places) for shift in range(places)]
 
     def mine():
         return pl.ds(pl.multiple_of(me * tile, tile), tile)
 
-    def exchange(source, target, group, signal):
-        def send(step, carry):
-            peer = peer_at(step)
+    def exchange(source, target, group_at, signal):
+        def send(outer, member, shift):
+            inner = near_places[shift] * group + member
+            start = pl.multiple_of((outer * inner_count + inner) * tile, tile)
             pltpu.make_async_remote_copy(
-                src_ref=source.at[signal, pl.ds(pl.multiple_of(peer * tile, tile), tile), :],
+                src_ref=source.at[signal, pl.ds(start, tile), :],
                 dst_ref=target.at[signal, mine(), :],
-                send_sem=send_sems.at[group, signal],
-                recv_sem=recv_sems.at[group, signal],
-                device_id=device(peer),
+                send_sem=send_sems.at[group_at, signal],
+                recv_sem=recv_sems.at[group_at, signal],
+                device_id=(outer, inner),
                 device_id_type=MESH,
             ).start()
+
+        def send_places(turn, carry):
+            outer = lax.rem(my_outer + turn, outer_count)
+            member = lax.rem(my_inner + lax.div(turn, outer_count), group)
+            for shift in (*range(places // 2, places), *range(places // 2)):
+                send(outer, member, shift)
             return carry
 
-        lax.fori_loop(1, devices, send, 0)
+        lax.fori_loop(1, planes, send_places, 0)
+        for shift in range(1, places):
+            send(my_outer, lax.rem(my_inner, group), shift)
         target[signal, mine(), :] = source[signal, mine(), :]
 
     def all_but_one(buffer, signal):

time: 52.3 us -> 52.3 us (level)
  no operation moved by 1% of the time
where the time goes in v2:
time: 52.3 us; the launch traced here: 52.1 us
  Pallas kernels  51.5 us (98%)
  between operations  0.64 us (1%)
    pallas_call x1, Pallas kernels, by_channel(): pl.pallas_call(functools.partial(kernel, outer_count, inner_count), out_s...  49.1 us
    pallas_call x1, Pallas kernels, by_channel(): pl.pallas_call(store_kernel, out_shape=tuple((jax.ShapeDtypeStruct(out.sh...  2.38 us

profile of v2, /device:TPU:0, one launch (start us, length us, event | category | flops | bytes accessed | tf_op | source)
XLA Modules:
  0.0 52.1 jit_solution(10661113510457348562)
XLA Ops:
  0.6 49.1 %shard_map.146 = (f32[512,128]{1,0:T(8,128)}, f32[3,512,128]{2,1,0:T(8,128)}, f32[512,128]{1,0:T(8,128)}, f32[3,3,128]{2,1,0:T(4,128)}, f32[1,128]{1,0:T(1,128)}) custom-call(f32[512,128]{1,0:T(8,128)} %query_hbm.1, f32[512,128]{1,0:T(8,128)} %key_hbm.1, f32[512,128]{1,0:T(8,128)} %value_hbm.1, f32[512,128]{1,0:T(8,128)} %taps_hbm.1, f32[1,128]{1,0:T(1,128)} %bitcast.2, ...), custom_call_target="tpu_custom_call" | custom-call | tf_op jit(solution)/shard_map/pallas_call | solution.py:692
  49.8 2.4 %shard_map.147 = (f32[512,128]{1,0:T(8,128)}, f32[3,512,128]{2,1,0:T(8,128)}, f32[512,128]{1,0:T(8,128)}, f32[3,3,128]{2,1,0:T(4,128)}, f32[1,128]{1,0:T(1,128)}) custom-call(f32[512,128]{1,0:T(8,128)} %get-tuple-element.15.refs_0_, f32[3,512,128]{2,1,0:T(8,128)} %get-tuple-element.16.refs_1_, f32[512,128]{1,0:T(8,128)} %get-tuple-element.17.refs_2_, ...), custom_call_target="tpu_custom_call" | custom-call | tf_op jit(solution)/shard_map/pallas_call | solution.py:744
